TPU v7x, 32 devices: a whole 2x2x4 slice. The times are simulated.
32 devices in a mesh: rows: 8 (over z, x), tensor: 4 (over y, core).
Axes of the slice: x: 2, y: 2, z: 4, core: 2. Of those that a mesh axis runs over, the one named last changes fastest.
Arguments:
- context: bfloat16 [2, 1280, 4096], P(None, 'rows', 'tensor'), may hold values from -6 to 6
- o_weight: bfloat16 [4096, 8192], P('tensor'), may hold values from -0.125 to 0.125
- residual: bfloat16 [2, 1280, 8192], P(None, 'rows', 'tensor'), may hold values from -6 to 6
- counts: int32 [2, 256], P(None, 'rows'), may hold values from 0 to 5
- slots: int32 [2, 1280], P(None, 'rows'), may hold values from 0 to 1279, as said below
- fc_weight: bfloat16 [2048, 8192], P('rows', 'tensor'), may hold values from -0.0625 to 0.0625
- gain: float32 [2048], replicated, may hold values from 0.1 to 1.9
- goal: bfloat16 [2, 1280, 2048], P(None, 'rows'), may hold values from -6 to 6
Outputs:
- verified: float32 [2, 1280, 8192], P(None, 'rows', 'tensor')
- draft_out: float32 [2, 1280, 2048], P(None, 'rows', 'tensor')
- fc_grad: float32 [2048, 8192], P('rows', 'tensor')
Inputs may be any that keep to these rules, and one draw needn't show every extreme that they name: In each step the slots of all rows are a permutation of 0 to 1279. Slot i belongs to trainer device i // 160; the rows of device p take, on every trainer device, exactly the 20 slots from p * 20 to (p + 1) * 20 - 1 of that device's block.
All inputs are finite; a program needn't handle non-finite values.
Results may differ from a plain program's by a relative error of at most 0.014.
Values may be sent and summed in bfloat16 or wider, within the bound.
A program may use at most 128 MiB of HBM per device.

v0:
```python
import math

import jax
import jax.numpy as jnp
from jax import lax
from jax.sharding import PartitionSpec as P

K = 5
STEPS = 2


epsilon = 1e-06


def draft_norm(summed, gain, goal, weight):
    mean_square = jnp.mean(summed * summed, axis=-1, keepdims=True)
    inverse = lax.rsqrt(mean_square + epsilon)
    normed = summed * inverse * gain
    error = normed - goal.astype(jnp.float32)
    pulled = gain * (weight * error)
    spread = jnp.mean(summed * pulled, axis=-1, keepdims=True)
    back = inverse * (pulled - summed * (inverse * inverse) * spread)
    return (normed, back.astype(jnp.bfloat16))


def grad_term(back_rows, input_rows):
    return lax.dot_general(
        back_rows, input_rows, (((0,), (0,)), ((), ())), preferred_element_type=jnp.float32
    )


def local(context, o_weight, residual, counts, slots, fc_weight, gain, goal):
    row_count = lax.axis_size("rows")
    rows_dev = context.shape[1]
    width = residual.shape[2]
    per_peer = rows_dev // row_count
    source = lax.axis_index("rows")
    weight = 1.0 / math.sqrt(STEPS * rows_dev * row_count)
    offsets = jnp.arange(rows_dev, dtype=jnp.int32) % K
    verified = []
    arrivals = []
    for step in range(STEPS):
        head_terms = jnp.dot(context[step], o_weight, preferred_element_type=jnp.float32)
        projected = lax.psum_scatter(
            head_terms.astype(jnp.bfloat16), "tensor", scatter_dimension=1, tiled=True
        ).astype(jnp.float32)
        full_state = residual[step].astype(jnp.float32) + projected
        verified.append(full_state)
        hidden = full_state.astype(jnp.bfloat16)
        accepted = offsets < jnp.repeat(counts[step], K)
        masked = jnp.where(accepted[:, None], hidden, jnp.zeros_like(hidden))
        slot_ids = slots[step]
        position = slot_ids // rows_dev * per_peer + slot_ids % rows_dev - source * per_peer
        outgoing = jnp.zeros_like(masked).at[position].set(masked)
        arrived = lax.all_to_all(
            outgoing.reshape(row_count, per_peer, width),
            "rows",
            split_axis=0,
            concat_axis=0,
            tiled=True,
        )
        arrivals.append(arrived.reshape(rows_dev, width))
    trained = jnp.concatenate(arrivals, 0)
    draft_terms = lax.dot_general(
        trained,
        lax.all_gather(fc_weight, "rows", axis=0, tiled=True),
        (((1,), (1,)), ((), ())),
        preferred_element_type=jnp.float32,
    )
    goal_rows = goal.reshape(STEPS * rows_dev, goal.shape[2])
    share = lax.psum_scatter(draft_terms, "tensor", scatter_dimension=0, tiled=True)
    share_rows = share.shape[0]
    goal_share = lax.dynamic_slice_in_dim(
        goal_rows, lax.axis_index("tensor") * share_rows, share_rows, 0
    )
    normed_share, back_share = draft_norm(share, gain, goal_share, weight)
    back = lax.all_gather(back_share, "tensor", axis=0, tiled=True)
    own_normed = lax.all_to_all(normed_share, "tensor", split_axis=1, concat_axis=0, tiled=True)
    grad = lax.psum_scatter(grad_term(back, trained), "rows", scatter_dimension=0, tiled=True)
    draft_out = own_normed.reshape(STEPS, rows_dev, own_normed.shape[1])
    return (jnp.stack(verified), draft_out, grad)


def solution(mesh):
    placed = (
        P(None, "rows", "tensor"),
        P("tensor", None),
        P(None, "rows", "tensor"),
        P(None, "rows"),
        P(None, "rows"),
        P("rows", "tensor"),
        P(),
        P(None, "rows", None),
    )
    return jax.shard_map(
        local,
        mesh=mesh,
        in_specs=placed,
        out_specs=(P(None, "rows", "tensor"), P(None, "rows", "tensor"), P("rows", "tensor")),
        check_vma=False,
    )
```

profile of v0, /device:TPU:0, one launch (start us, length us, event | category | flops | bytes accessed | tf_op | source)
XLA Modules:
  0.0 551.8 jit_solution(2388277677716777111)
XLA Ops:
  8.0 10.3 %convolution_convert_fusion.1 = bf16[160,8192]{1,0:T(8,128)(2,1)} fusion(bf16[1024,8192]{1,0:T(8,128)(2,1)} %param.9, bf16[2,160,1024]{2,1,0:T(8,128)(2,1)} %param.8), kind=kOutput, calls=%fused_computation.3 | convolution fusion | flops 2685665280 | bytes 19726336 | tf_op jit(solution)/shard_map/dot_general | solution.py:43
  18.4 1.0 copy-done.5
  19.4 10.2 %convolution_convert_fusion = bf16[160,8192]{1,0:T(8,128)(2,1)} fusion(bf16[1024,8192]{1,0:T(8,128)(2,1)} %param.9, bf16[2,160,1024]{2,1,0:T(8,128)(2,1)S(1)} %copy-done.5), kind=kOutput, calls=%fused_computation.2 | convolution fusion | flops 2685665280 | bytes 19726336 | tf_op jit(solution)/shard_map/dot_general | solution.py:43
  29.7 0.5 all-gather.3.cloned.1.call-update
  30.5 25.3 %reduce-scatter.5.cloned.1.call-done = bf16[160,2048]{1,0:T(8,128)(2,1)} async-done(((bf16[160,8192]{1,0:T(8,128)(2,1)}), bf16[160,2048]{1,0:T(8,128)(2,1)}) %reduce-scatter.5.cloned.1.call-update) | async-done | bytes 655376 | tf_op jit(solution)/shard_map/reduce_scatter | solution.py:44
  55.9 2.4 scatter_custom_fusion
  58.3 1.0 reshape.237
  59.3 5.5 all-to-all-start
  65.0 28.3 %reduce-scatter.7.cloned.1.call-done = bf16[160,2048]{1,0:T(8,128)(2,1)} async-done(((bf16[160,8192]{1,0:T(8,128)(2,1)}), bf16[160,2048]{1,0:T(8,128)(2,1)}) %reduce-scatter.7.cloned.1.call-update) | async-done | bytes 655376 | tf_op jit(solution)/shard_map/reduce_scatter | solution.py:44
  93.3 2.4 scatter_custom_fusion.1
  95.7 1.0 reshape.240
  96.7 1.6 all-to-all-done
  98.3 3.9 all-to-all-start.1
  102.6 42.3 %all-to-all-done.1 = bf16[8,20,2048]{2,1,0:T(8,128)(2,1)S(1)} async-done(((bf16[8,20,2048]{2,1,0:T(8,128)(2,1)}), bf16[8,20,2048]{2,1,0:T(8,128)(2,1)S(1)}, u32[]{:S(2)}, u32[]{:S(2)}) %all-to-all-start.1) | async-done | bytes 655392 | tf_op jit(solution)/shard_map/all_to_all | solution.py:55
  144.9 1.0 reshape.241
  145.9 1.0 copy-done.4
  147.0 42.5 %all-gather.3.cloned.1.call-done = bf16[2048,2048]{1,0:T(8,128)(2,1)} async-done(((bf16[256,2048]{1,0:T(8,128)(2,1)}), bf16[2048,2048]{1,0:T(8,128)(2,1)}) %all-gather.3.cloned.1.call-update) | async-done | bytes 8388624 | tf_op jit(solution)/shard_map/all_gather | solution.py:66
  189.5 7.8 %fusion.25 = f32[320,2048]{1,0:T(8,128)} fusion(bf16[320,2048]{1,0:T(8,128)(2,1)S(1)} %constant_dynamic-update-slice_fusion, bf16[2048,2048]{1,0:T(8,128)(2,1)} %all-gather.3.cloned.1.call-done), kind=kOutput, calls=%fused_computation.50 | convolution fusion | flops 2684354560 | bytes 12320768 | tf_op jit(solution)/shard_map/dot_general | solution.py:64
  197.3 0.6 copy-done.6
  197.9 33.2 %reduce-scatter.9.cloned.1.call-done = f32[80,2048]{1,0:T(8,128)} async-done(((f32[320,2048]{1,0:T(8,128)}), f32[80,2048]{1,0:T(8,128)}) %reduce-scatter.9.cloned.1.call-update) | async-done | bytes 655376 | tf_op jit(solution)/shard_map/reduce_scatter | solution.py:71
  231.1 1.3 multiply_reduce_fusion.1
  232.4 1.5 multiply_reduce_fusion
  233.9 2.0 multiply_convert_fusion
  236.0 18.3 %all-gather.5.cloned.1.call-done = bf16[320,2048]{1,0:T(8,128)(2,1)} async-done(((bf16[80,2048]{1,0:T(8,128)(2,1)}), bf16[320,2048]{1,0:T(8,128)(2,1)}) %all-gather.5.cloned.1.call-update) | async-done | bytes 1310736 | tf_op jit(solution)/shard_map/all_gather | solution.py:77
  254.3 9.5 %fusion.26 = f32[2048,2048]{1,0:T(8,128)} fusion(bf16[320,2048]{1,0:T(8,128)(2,1)} %all-gather.5.cloned.1.call-done, bf16[320,2048]{1,0:T(8,128)(2,1)S(1)} %constant_dynamic-update-slice_fusion), kind=kOutput, calls=%fused_computation.51 | convolution fusion | flops 2684354560 | bytes 19398656 | tf_op jit(solution)/shard_map/dot_general | solution.py:27
  263.9 0.9 copy.16
  264.8 3.5 all-to-all-start.2
  268.3 0.5 fusion.1
  268.8 1.7 pad_maximum_fusion
  270.5 8.0 %all-to-all-done.2 = f32[80,4,512]{2,0,1:T(8,128)S(1)} async-done(((f32[80,4,512]{2,0,1:T(8,128)}), f32[80,4,512]{2,0,1:T(8,128)S(1)}, u32[]{:S(2)}, u32[]{:S(2)}) %all-to-all-start.2) | async-done | bytes 655392 | tf_op jit(solution)/shard_map/all_to_all | solution.py:78
  278.5 265.4 %reduce-scatter.11.cloned.1.call-done = f32[256,2048]{1,0:T(8,128)} async-done(((f32[2048,2048]{1,0:T(8,128)}), f32[256,2048]{1,0:T(8,128)}) %reduce-scatter.11.cloned.1.call-update) | async-done | bytes 2097168 | tf_op jit(solution)/shard_map/reduce_scatter | solution.py:79
  543.9 0.8 copy.19
  (40 shorter events, 1.3 us)
Async XLA Ops:
  8.0 47.9 %reduce-scatter.5.cloned.1.call-start = ((), (), s32[]{:S(2)}) async-start(), calls=%async_computation.7 | async-start | bytes 3276800 | tf_op jit(solution)/shard_map/reduce_scatter | solution.py:44
  18.3 1.1 copy-start.5
  18.3 74.9 %reduce-scatter.7.cloned.1.call-start = ((), (), s32[]{:S(2)}) async-start(), calls=%async_computation.8 | async-start | bytes 3276800 | tf_op jit(solution)/shard_map/reduce_scatter | solution.py:44
  29.6 0.7 copy-start.8
  29.6 0.9 copy-start.7
  29.6 26.3 %copy-start.1 = (bf16[2,160,2048]{2,1,0:T(8,128)(2,1)S(1)}, bf16[2,160,2048]{2,1,0:T(8,128)(2,1)}, u32[]{:S(2)}) copy-start(bf16[2,160,2048]{2,1,0:T(8,128)(2,1)} %param.10) | copy-start | bytes 3932164
  29.7 159.8 %all-gather.3.cloned.1.call-start = ((), (), s32[]{:S(2)}) async-start(), calls=%async_computation.9 | async-start | bytes 9437184 | tf_op jit(solution)/shard_map/all_gather | solution.py:66
  59.3 39.0 %all-to-all-start = ((bf16[8,20,2048]{2,1,0:T(8,128)(2,1)}), bf16[8,20,2048]{2,1,0:T(8,128)(2,1)S(1)}, u32[]{:S(2)}, u32[]{:S(2)}) async-start(bf16[8,20,2048]{2,1,0:T(8,128)(2,1)} %reshape.237), calls=%async_computation.2 | async-start | bytes 1572864 | tf_op jit(solution)/shard_map/all_to_all | solution.py:55
  98.3 46.6 %all-to-all-start.1 = ((bf16[8,20,2048]{2,1,0:T(8,128)(2,1)}), bf16[8,20,2048]{2,1,0:T(8,128)(2,1)S(1)}, u32[]{:S(2)}, u32[]{:S(2)}) async-start(bf16[8,20,2048]{2,1,0:T(8,128)(2,1)} %reshape.240), calls=%async_computation.3 | async-start | bytes 1572864 | tf_op jit(solution)/shard_map/all_to_all | solution.py:55
  102.2 128.9 %reduce-scatter.9.cloned.1.call-start = ((), (), s32[]{:S(2)}) async-start(), calls=%async_computation.10 | async-start | bytes 3276800 | tf_op jit(solution)/shard_map/reduce_scatter | solution.py:71
  145.9 1.1 copy-start.4
  197.2 0.7 copy-start.6
  197.3 57.1 %all-gather.5.cloned.1.call-start = ((), (), s32[]{:S(2)}) async-start(), calls=%async_computation.11 | async-start | bytes 1638400 | tf_op jit(solution)/shard_map/all_gather | solution.py:77
  231.1 2.8 copy-start
  236.0 307.9 %reduce-scatter.11.cloned.1.call-start = ((), (), s32[]{:S(2)}) async-start(), calls=%async_computation.12 | async-start | bytes 18874368 | tf_op jit(solution)/shard_map/reduce_scatter | solution.py:79
  263.9 4.4 copy-start.2
  263.9 4.4 copy-start.3
  264.8 13.7 %all-to-all-start.2 = ((f32[80,4,512]{2,0,1:T(8,128)}), f32[80,4,512]{2,0,1:T(8,128)S(1)}, u32[]{:S(2)}, u32[]{:S(2)}) async-start(f32[80,4,512]{2,0,1:T(8,128)} %bitcast.84), calls=%async_computation.5 | async-start | bytes 1310720 | tf_op jit(solution)/shard_map/all_to_all | solution.py:78
Sparse Core Ops, SparseCore 0:
  18.5 37.3 reduce-scatter.4
  58.6 34.6 reduce-scatter.6
  197.4 33.6 reduce-scatter.8
  236.1 18.1 all-gather.4
Sparse Core Ops, SparseCore 1:
  32.3 157.2 all-gather.2
  264.0 279.8 reduce-scatter.10
where the time goes:
time: 553 us; the launch traced here: 552 us
  waiting for transfers between devices  466 us (84%)
  matrix products  37.8 us (7%)
  between operations  15.4 us (3%)
  starting transfers between devices  13.3 us (2%)
  other arithmetic  11.8 us (2%)
  local copies, waits for them, and re-layouts  8.05 us (1%)
    reduce_scatter x1, waiting for transfers between devices, local(): lax.psum_scatter(grad_term(back, trained), 'rows', scatter_dimension=0, t...  265 us
    reduce_scatter x2, waiting for transfers between devices, local(): lax.psum_scatter(head_terms.astype(jnp.bfloat16), 'tensor', scatter_dimen...  53.6 us
    all_to_all x2, waiting for transfers between devices, local(): lax.all_to_all(outgoing.reshape(row_count, per_peer, width), 'rows', spli...  44 us
    all_gather x1, waiting for transfers between devices, local(): lax.all_gather(fc_weight, 'rows', axis=0, tiled=True)  42.5 us
    reduce_scatter x1, waiting for transfers between devices, local(): lax.psum_scatter(draft_terms, 'tensor', scatter_dimension=0, tiled=True)  33.2 us
    dot_general x2, matrix products, local(): jnp.dot(context[step], o_weight, preferred_element_type=jnp.float32)  20.5 us
    all_gather x1, waiting for transfers between devices, local(): back = lax.all_gather(back_share, 'tensor', axis=0, tiled=True)  18.3 us
  transfers between devices with their start and end apart: 9, of which 9 were waited for; matrix products, arithmetic and copies ran while one was open for 4% of the time, Pallas kernels for 0%

commit v1 on v0

v1 whole, which is shorter than its diff:
```python
import math

import jax
import jax.numpy as jnp
from jax import lax
from jax.sharding import PartitionSpec as P

K = 5
epsilon = 1e-06


def local(context, o_weight, residual, counts, slots, fc_weight, gain, goal):
    steps = context.shape[0]
    row_count = lax.axis_size("rows")
    inner = lax.axis_size("tensor")
    outer = row_count // inner
    rows_dev = context.shape[1]
    width = residual.shape[2]
    block = fc_weight.shape[0]
    draft = goal.shape[2]
    per_peer = rows_dev // row_count
    source = lax.axis_index("rows")
    column = lax.axis_index("tensor")
    hi = source // inner
    lo = source % inner
    weight = 1.0 / math.sqrt(steps * rows_dev * row_count)
    groups = [[h * inner + l for l in range(inner)] for h in range(outer)]
    shifts = [
        [(r, (r + k * inner) % row_count) for r in range(row_count)] for k in range(outer)
    ]

    weights = [fc_weight] + [lax.ppermute(fc_weight, "rows", shifts[k]) for k in range(1, outer)]
    weights = jnp.concatenate(weights, 0)
    relative = (jnp.arange(outer)[:, None] - jnp.arange(outer)[None, :]) % outer
    goal_part = lax.dynamic_index_in_dim(
        goal.reshape(steps, outer, inner, per_peer, outer, inner, block), column, 2, False
    )
    goal_out = jnp.stack(
        [
            jnp.stack([goal_part[:, h, :, (h - k) % outer] for k in range(outer)], 2)
            for h in range(outer)
        ],
        0,
    )
    goal_out = jnp.transpose(goal_out, (0, 4, 1, 2, 3, 5)).reshape(
        row_count, steps, per_peer, outer * block
    )
    goal_in = lax.all_to_all(goal_out, "rows", split_axis=0, concat_axis=0, tiled=True)
    goal_in = jnp.transpose(goal_in, (1, 0, 2, 3)).reshape(steps * rows_dev, outer * block)
    gain_own = gain.reshape(outer, inner, block)[relative[hi], lo].reshape(1, outer * block)

    offsets = jnp.arange(rows_dev, dtype=jnp.int32) % K
    verified = []
    hidden_rows = []
    for step in range(steps):
        head_terms = jnp.dot(context[step], o_weight, preferred_element_type=jnp.float32)
        projected = lax.psum_scatter(
            head_terms.astype(jnp.bfloat16), "tensor", scatter_dimension=1, tiled=True
        ).astype(jnp.float32)
        full_state = residual[step].astype(jnp.float32) + projected
        verified.append(full_state)
        hidden = full_state.astype(jnp.bfloat16)
        accepted = offsets < jnp.repeat(counts[step], K)
        slot_ids = slots[step]
        position = slot_ids // rows_dev * per_peer + slot_ids % rows_dev - source * per_peer
        place = (position[None, :] == jnp.arange(rows_dev)[:, None]) & accepted[None, :]
        moved = jnp.dot(
            place.astype(jnp.bfloat16), hidden, preferred_element_type=jnp.float32
        ).astype(jnp.bfloat16)
        hidden_rows.append(
            lax.all_gather(moved, "rows", axis=0, tiled=False, axis_index_groups=groups)
        )
    trained = jnp.stack(hidden_rows, 1).reshape(inner * steps * rows_dev, width)
    terms = lax.dot_general(
        trained, weights, (((1,), (1,)), ((), ())), preferred_element_type=jnp.float32
    ).astype(jnp.bfloat16)
    summed = lax.psum_scatter(terms, "tensor", scatter_dimension=0, tiled=True).astype(jnp.float32)
    goal_rows = goal_in.astype(jnp.float32)
    scaled = summed * gain_own
    stats = jnp.stack(
        [
            jnp.sum(summed * summed, -1),
            jnp.sum(scaled * scaled, -1),
            jnp.sum(scaled * goal_rows, -1),
        ]
    )
    stats = jnp.sum(
        lax.all_gather(stats, "rows", axis=0, tiled=False, axis_index_groups=groups), 0
    )
    inverse = lax.rsqrt(stats[0] / draft + epsilon)
    spread = weight * (inverse * stats[1] - stats[2]) / draft
    inverse = inverse[:, None]
    spread = spread[:, None]
    normed = scaled * inverse
    pulled = gain_own * (weight * (normed - goal_rows))
    back_share = (inverse * (pulled - summed * (inverse * inverse) * spread)).astype(jnp.bfloat16)
    back = lax.all_gather(back_share, "tensor", axis=0, tiled=True)
    grad_terms = []
    for k in range(outer):
        grad_terms.append(
            lax.dot_general(
                back[:, k * block : (k + 1) * block],
                trained,
                (((0,), (0,)), ((), ())),
                preferred_element_type=jnp.float32,
            )
        )
    grad = grad_terms[0]
    for k in range(1, outer):
        back_shift = [(b, a) for a, b in shifts[k]]
        grad = grad + lax.ppermute(
            grad_terms[k].astype(jnp.bfloat16), "rows", back_shift
        ).astype(jnp.float32)

    out = normed.astype(jnp.bfloat16).reshape(steps, row_count, per_peer, outer * block)
    out = lax.all_to_all(
        jnp.transpose(out, (1, 0, 2, 3)), "rows", split_axis=0, concat_axis=0, tiled=True
    ).reshape(outer, inner, steps, per_peer, outer, block)
    out = jnp.stack(
        [
            jnp.stack([out[h, :, :, :, (h - a) % outer] for a in range(outer)], 0)
            for h in range(outer)
        ],
        0,
    )
    out = jnp.transpose(out, (1, 2, 5, 3, 0, 4))
    out = jnp.transpose(
        out.reshape(inner, draft // inner, steps, outer, per_peer), (0, 2, 3, 4, 1)
    )
    out = lax.all_to_all(out, "tensor", split_axis=0, concat_axis=0, tiled=True)
    draft_out = (
        jnp.transpose(out, (1, 2, 0, 3, 4))
        .reshape(steps, rows_dev, draft // inner)
        .astype(jnp.float32)
    )
    return (jnp.stack(verified), draft_out, grad)


def solution(mesh):
    placed = (
        P(None, "rows", "tensor"),
        P("tensor", None),
        P(None, "rows", "tensor"),
        P(None, "rows"),
        P(None, "rows"),
        P("rows", "tensor"),
        P(),
        P(None, "rows", None),
    )
    return jax.shard_map(
        local,
        mesh=mesh,
        in_specs=placed,
        out_specs=(P(None, "rows", "tensor"), P(None, "rows", "tensor"), P("rows", "tensor")),
        check_vma=False,
    )
```

time: 553 us -> 341 us (0.62)
  waiting for transfers between devices: 466 us -> 229 us
  blocking collectives: 0 us -> 11.5 us
  local copies, waits for them, and re-layouts: 8.05 us -> 14.9 us
    reduce_scatter x2 -> x1, waiting for transfers between devices: 299 us -> 6.84 us  [local(): lax.psum_scatter(terms, 'tensor', scatter_dimension=0, tiled=True)]
    all_gather x1 -> x2, waiting for transfers between devices: 42.5 us -> 106 us  [local(): lax.all_gather(moved, 'rows', axis=0, tiled=False, axis_index_groups=groups)]
    ppermute x0 -> x2, waiting for transfers between devices: none -> 31.5 us  [the longest x1 31.5 us: local(): lax.ppermute(grad_terms[k].astype(jnp.bfloat16), 'rows', back_shift)]
    all_to_all x3, waiting for transfers between devices: 52 us -> 21.4 us  [the longest x1 9.71 us: local(): lax.all_to_all(goal_out, 'rows', split_axis=0, concat_axis=0, tiled=True)]
    all_gather x1, waiting for transfers between devices: 18.3 us -> 1.75 us  [local(): back = lax.all_gather(back_share, 'tensor', axis=0, tiled=True)]
    all_gather x0 -> x1, blocking collectives: none -> 11.5 us  [local(): lax.all_gather(stats, 'rows', axis=0, tiled=False, axis_index_groups=groups)]
    reduce_scatter x2, waiting for transfers between devices: 53.6 us -> 60.8 us  [local(): lax.psum_scatter(head_terms.astype(jnp.bfloat16), 'tensor', scatter_dimen...]
    dot_general x2 -> x5, matrix products: 17.3 us -> 19.4 us  [the longest x2 10.8 us: local(): lax.dot_general(back[:, k * block:(k + 1) * block], trained, (((0,), (0,)...]
  transfers between devices with their start and end apart: 9 -> 11, of which waited for: 9 -> 10; matrix products, arithmetic and copies ran while one was open for 4% -> 10% of each run, Pallas kernels for 0% -> 0%
where the time goes in v1:
time: 341 us; the launch traced here: 340 us
  waiting for transfers between devices  229 us (67%)
  matrix products  39.9 us (12%)
  starting transfers between devices  18.3 us (5%)
  local copies, waits for them, and re-layouts  14.9 us (4%)
  between operations  14.5 us (4%)
  other arithmetic  12.1 us (4%)
  blocking collectives  11.5 us (3%)
    all_gather x2, waiting for transfers between devices, local(): lax.all_gather(moved, 'rows', axis=0, tiled=False, axis_index_groups=groups)  106 us
    reduce_scatter x2, waiting for transfers between devices, local(): lax.psum_scatter(head_terms.astype(jnp.bfloat16), 'tensor', scatter_dimen...  60.8 us
    ppermute x1, waiting for transfers between devices, local(): lax.ppermute(grad_terms[k].astype(jnp.bfloat16), 'rows', back_shift)  31.5 us
    dot_general x2, matrix products, local(): jnp.dot(context[step], o_weight, preferred_element_type=jnp.float32)  20.4 us
    all_gather x1, blocking collectives, local(): lax.all_gather(stats, 'rows', axis=0, tiled=False, axis_index_groups=groups)  11.5 us
    dot_general x2, matrix products, local(): lax.dot_general(back[:, k * block:(k + 1) * block], trained, (((0,), (0,)...  10.8 us
    all_to_all x1, waiting for transfers between devices, local(): lax.all_to_all(goal_out, 'rows', split_axis=0, concat_axis=0, tiled=True)  9.71 us
    reduce_scatter x1, waiting for transfers between devices, local(): lax.psum_scatter(terms, 'tensor', scatter_dimension=0, tiled=True)  6.84 us
  transfers between devices with their start and end apart: 11, of which 10 were waited for; matrix products, arithmetic and copies ran while one was open for 10% of the time, Pallas kernels for 0%

profile of v1, /device:TPU:0, one launch (start us, length us, event | category | flops | bytes accessed | tf_op | source)
XLA Modules:
  0.0 339.7 jit_solution(8108835980582947840)
XLA Ops:
  7.2 10.3 %convolution_convert_fusion = bf16[160,8192]{1,0:T(8,128)(2,1)} fusion(bf16[1024,8192]{1,0:T(8,128)(2,1)} %param.9, bf16[2,160,1024]{2,1,0:T(8,128)(2,1)} %param.8), kind=kOutput, calls=%fused_computation.1 | convolution fusion | flops 2685665280 | bytes 19726336 | tf_op jit(solution)/shard_map/dot_general | solution.py:56
  18.6 10.2 %convolution_convert_fusion.1 = bf16[160,8192]{1,0:T(8,128)(2,1)} fusion(bf16[1024,8192]{1,0:T(8,128)(2,1)} %param.9, bf16[2,160,1024]{2,1,0:T(8,128)(2,1)S(1)} %copy-done.5), kind=kOutput, calls=%fused_computation.2 | convolution fusion | flops 2685665280 | bytes 19726336 | tf_op jit(solution)/shard_map/dot_general | solution.py:56
  29.7 25.4 %reduce-scatter.6.cloned.1.call-done = bf16[160,2048]{1,0:T(8,128)(2,1)} async-done(((bf16[160,8192]{1,0:T(8,128)(2,1)}), bf16[160,2048]{1,0:T(8,128)(2,1)}) %reduce-scatter.6.cloned.1.call-update) | async-done | bytes 655376 | tf_op jit(solution)/shard_map/reduce_scatter | solution.py:57
  55.0 2.3 convolution_convert_fusion.4
  57.6 35.4 %reduce-scatter.4.cloned.1.call-done = bf16[160,2048]{1,0:T(8,128)(2,1)} async-done(((bf16[160,8192]{1,0:T(8,128)(2,1)}), bf16[160,2048]{1,0:T(8,128)(2,1)}) %reduce-scatter.4.cloned.1.call-update) | async-done | bytes 655376 | tf_op jit(solution)/shard_map/reduce_scatter | solution.py:57
  93.0 2.3 convolution_convert_fusion.5
  95.4 2.5 collective-permute-start
  97.8 51.2 %all-gather.12.cloned.1.call-done = bf16[640,2048]{1,0:T(8,128)(2,1)} async-done(((bf16[160,2048]{1,0:T(8,128)(2,1)}), bf16[640,2048]{1,0:T(8,128)(2,1)}) %all-gather.12.cloned.1.call-update) | async-done | bytes 2621456 | tf_op jit(solution)/shard_map/all_gather | solution.py:71
  149.0 55.2 %all-gather.10.cloned.1.call-done = bf16[640,2048]{1,0:T(8,128)(2,1)} async-done(((bf16[160,2048]{1,0:T(8,128)(2,1)}), bf16[640,2048]{1,0:T(8,128)(2,1)}) %all-gather.10.cloned.1.call-update) | async-done | bytes 2621456 | tf_op jit(solution)/shard_map/all_gather | solution.py:71
  204.2 3.0 pad_maximum_fusion
  207.2 2.3 copy-done
  209.5 4.0 %convolution_convert_fusion.2 = bf16[1280,512]{1,0:T(8,128)(2,1)} fusion(bf16[1280,2048]{1,0:T(8,128)(2,1)S(1)} %bitcast.103, bf16[256,2048]{1,0:T(8,128)(2,1)S(1)} %collective-permute-done, bf16[256,2048]{1,0:T(8,128)(2,1)S(1)} %copy-done.9), kind=kOutput, calls=%fused_computation.4 | convolution fusion | flops 2689204224 | bytes 8650752 | tf_op jit(solution)/shard_map/dot_general | solution.py:74
  213.5 1.3 copy-done.3
  217.9 4.2 %all-to-all-start = ((bf16[8,2,20,512]{3,1,2,0:T(2,128)(2,1)}), bf16[8,2,20,512]{3,1,2,0:T(2,128)(2,1)S(1)}, u32[]{:S(2)}, u32[]{:S(2)}) async-start(bf16[8,2,20,512]{3,1,2,0:T(2,128)(2,1)} %reshape.152), calls=%async_computation.3 | async-start | bytes 655360 | tf_op jit(solution)/shard_map/all_to_all | solution.py:48
  222.8 9.7 %all-to-all-done = bf16[8,2,20,512]{3,1,2,0:T(2,128)(2,1)S(1)} async-done(((bf16[8,2,20,512]{3,1,2,0:T(2,128)(2,1)}), bf16[8,2,20,512]{3,1,2,0:T(2,128)(2,1)S(1)}, u32[]{:S(2)}, u32[]{:S(2)}) %all-to-all-start) | async-done | bytes 327712 | tf_op jit(solution)/shard_map/all_to_all | solution.py:48
  233.0 6.8 %reduce-scatter.8.cloned.1.call-done = bf16[320,512]{1,0:T(8,128)(2,1)} async-done(((bf16[1280,512]{1,0:T(8,128)(2,1)}), bf16[320,512]{1,0:T(8,128)(2,1)}) %reduce-scatter.8.cloned.1.call-update) | async-done | bytes 327696 | tf_op jit(solution)/shard_map/reduce_scatter | solution.py:77
  239.8 1.3 fusion.16
  241.2 11.5 %all-gather.3 = f32[4,3,320]{2,1,0:T(4,128)S(1)} all-gather(f32[1,3,320]{2,1,0:T(4,128)S(1)} %maximum_bitcast_fusion.6), channel_id=4, replica_groups={{0,4,8,12},{16,20,24,28},{1,5,9,13},{17,21,25,29},{2,6,10,14},{18,22,26..., dimensions={0}, use_global_device_ids=true | all-gather | bytes 19200 | tf_op jit(solution)/shard_map/all_gather | solution.py:88
  252.7 2.0 fusion.15
  254.8 1.1 copy.105
  255.9 5.4 %all-to-all-start.1 = ((bf16[8,2,20,512]{3,1,2,0:T(2,128)(2,1)}), bf16[8,2,20,512]{3,1,2,0:T(2,128)(2,1)}, u32[]{:S(2)}, u32[]{:S(2)}) async-start(bf16[8,2,20,512]{3,1,2,0:T(2,128)(2,1)} %copy.105), calls=%async_computation.4 | async-start | bytes 655360 | tf_op jit(solution)/shard_map/all_to_all | solution.py:116
  261.3 2.1 fusion.4
  263.5 6.6 %all-to-all-done.1 = bf16[8,2,20,512]{3,1,2,0:T(2,128)(2,1)} async-done(((bf16[8,2,20,512]{3,1,2,0:T(2,128)(2,1)}), bf16[8,2,20,512]{3,1,2,0:T(2,128)(2,1)}, u32[]{:S(2)}, u32[]{:S(2)}) %all-to-all-start.1) | async-done | bytes 327712 | tf_op jit(solution)/shard_map/all_to_all | solution.py:116
  270.1 1.2 reshape.153
  271.3 1.8 all-gather.8.cloned.1.call-done
  273.0 5.2 %convolution_convert_fusion.3 = bf16[256,2048]{1,0:T(8,128)(2,1)} fusion(bf16[1280,2048]{1,0:T(8,128)(2,1)} %bitcast.104, bf16[1280,512]{1,0:T(8,128)(2,1)} %all-gather.8.cloned.1.call-done), kind=kOutput, calls=%fused_computation.6 | convolution fusion | flops 1342701568 | bytes 6946816 | tf_op jit(solution)/shard_map/dot_general | solution.py:101
  278.2 2.4 collective-permute-start.1
  283.9 3.5 %all-to-all-start.2 = ((bf16[4,2,2,20,512]{4,2,3,1,0:T(2,128)(2,1)}), bf16[4,2,2,20,512]{4,2,3,1,0:T(2,128)(2,1)S(1)}, u32[]{:S(2)}, u32[]{:S(2)}) async-start(bf16[4,2,2,20,512]{4,2,3,1,0:T(2,128)(2,1)} %copy.112), calls=%async_computation.5 | async-start | bytes 655360 | tf_op jit(solution)/shard_map/all_to_all | solution.py:130
  287.3 1.7 pad_maximum_fusion.1
  289.0 5.0 %all-to-all-done.2 = bf16[4,2,2,20,512]{4,2,3,1,0:T(2,128)(2,1)S(1)} async-done(((bf16[4,2,2,20,512]{4,2,3,1,0:T(2,128)(2,1)}), bf16[4,2,2,20,512]{4,2,3,1,0:T(2,128)(2,1)S(1)}, u32[]{:S(2)}, u32[]{:S(2)}) %all-to-all-start.2) | async-done | bytes 327712 | tf_op jit(solution)/shard_map/all_to_all | solution.py:130
  295.7 31.5 %collective-permute-done.1 = bf16[256,2048]{1,0:T(8,128)(2,1)} collective-permute-done((bf16[256,2048]{1,0:T(8,128)(2,1)}, bf16[256,2048]{1,0:T(8,128)(2,1)}, u32[]{:S(2)}, u32[]{:S(2)}) %collective-permute-start.1) | collective-permute-done | bytes 1048608 | tf_op jit(solution)/shard_map/ppermute | solution.py:111
  327.2 5.6 %convert_add_fusion = f32[256,2048]{1,0:T(8,128)} fusion(bf16[256,2048]{1,0:T(8,128)(2,1)} %collective-permute-done.1, bf16[1280,2048]{1,0:T(8,128)(2,1)} %bitcast.105, bf16[1280,512]{1,0:T(8,128)(2,1)S(1)} %copy-done.4), kind=kOutput, calls=%fused_computation.12 | convolution fusion | flops 1343225856 | bytes 9043968 | tf_op jit(solution)/shard_map/dot_general | solution.py:101
  (77 shorter events, 11.4 us)
Async XLA Ops:
  7.2 47.9 %reduce-scatter.6.cloned.1.call-start = ((), (), s32[]{:S(2)}) async-start(), calls=%async_computation.7 | async-start | bytes 3276800 | tf_op jit(solution)/shard_map/reduce_scatter | solution.py:57
  17.5 1.1 copy-start.5
  17.5 75.5 %reduce-scatter.4.cloned.1.call-start = ((), (), s32[]{:S(2)}) async-start(), calls=%async_computation.6 | async-start | bytes 3276800 | tf_op jit(solution)/shard_map/reduce_scatter | solution.py:57
  28.7 0.7 copy-start.8
  28.7 0.9 copy-start.7
  28.7 26.3 %copy-start.1 = (bf16[2,160,2048]{2,1,0:T(8,128)(2,1)S(1)}, bf16[2,160,2048]{2,1,0:T(8,128)(2,1)}, u32[]{:S(2)}) copy-start(bf16[2,160,2048]{2,1,0:T(8,128)(2,1)} %param.10) | copy-start | bytes 3932164
  28.8 120.2 %all-gather.12.cloned.1.call-start = ((), (), s32[]{:S(2)}) async-start(), calls=%async_computation.11 | async-start | bytes 3276800 | tf_op jit(solution)/shard_map/all_gather | solution.py:71
  57.3 38.0 %copy-start.9 = (bf16[256,2048]{1,0:T(8,128)(2,1)S(1)}, bf16[256,2048]{1,0:T(8,128)(2,1)}, u32[]{:S(2)}) copy-start(bf16[256,2048]{1,0:T(8,128)(2,1)} %param.13) | copy-start | bytes 3145732
  57.4 146.8 %all-gather.10.cloned.1.call-start = ((), (), s32[]{:S(2)}) async-start(), calls=%async_computation.10 | async-start | bytes 3276800 | tf_op jit(solution)/shard_map/all_gather | solution.py:71
  95.3 144.6 %reduce-scatter.8.cloned.1.call-start = ((), (), s32[]{:S(2)}) async-start(), calls=%async_computation.8 | async-start | bytes 1638400 | tf_op jit(solution)/shard_map/reduce_scatter | solution.py:77
  95.4 111.8 %collective-permute-start = (bf16[256,2048]{1,0:T(8,128)(2,1)S(1)}, bf16[256,2048]{1,0:T(8,128)(2,1)S(1)}, u32[]{:S(2)}, u32[]{:S(2)}) collective-permute-start(bf16[256,2048]{1,0:T(8,128)(2,1)S(1)} %copy-done.9), channel_id=1, source_target_pairs={{0,16},{4,20},{8,24},{12,28},{16,0},{20,4},{24,8},{28,12},{1,17},{... | collective-permute-start | bytes 3145736 | tf_op jit(solution)/shard_map/ppermute | solution.py:32
  207.2 2.3 copy-start
  213.5 1.3 copy-start.3
  216.0 6.2 %copy-start.6 = (f32[2048]{0:T(1024)S(1)}, f32[2048]{0:T(1024)}, u32[]{:S(2)}) copy-start(f32[2048]{0:T(1024)} %param.14) | copy-start | bytes 24580
  217.9 14.7 %all-to-all-start = ((bf16[8,2,20,512]{3,1,2,0:T(2,128)(2,1)}), bf16[8,2,20,512]{3,1,2,0:T(2,128)(2,1)S(1)}, u32[]{:S(2)}, u32[]{:S(2)}) async-start(bf16[8,2,20,512]{3,1,2,0:T(2,128)(2,1)} %reshape.152), calls=%async_computation.3 | async-start | bytes 655360 | tf_op jit(solution)/shard_map/all_to_all | solution.py:48
  222.1 50.9 %all-gather.8.cloned.1.call-start = ((), (), s32[]{:S(2)}) async-start(), calls=%async_computation.9 | async-start | bytes 1638400 | tf_op jit(solution)/shard_map/all_gather | solution.py:97
  241.1 20.2 %copy-start.2 = (bf16[160,2048]{1,0:T(8,128)(2,1)S(1)}, bf16[160,2048]{1,0:T(8,128)(2,1)}, u32[]{:S(2)}) copy-start(bf16[160,2048]{1,0:T(8,128)(2,1)} %reduce-scatter.6.cloned.1.call-done) | copy-start | bytes 1966084
  255.9 14.2 %all-to-all-start.1 = ((bf16[8,2,20,512]{3,1,2,0:T(2,128)(2,1)}), bf16[8,2,20,512]{3,1,2,0:T(2,128)(2,1)}, u32[]{:S(2)}, u32[]{:S(2)}) async-start(bf16[8,2,20,512]{3,1,2,0:T(2,128)(2,1)} %copy.105), calls=%async_computation.4 | async-start | bytes 655360 | tf_op jit(solution)/shard_map/all_to_all | solution.py:116
  278.2 49.0 %collective-permute-start.1 = (bf16[256,2048]{1,0:T(8,128)(2,1)}, bf16[256,2048]{1,0:T(8,128)(2,1)}, u32[]{:S(2)}, u32[]{:S(2)}) collective-permute-start(bf16[256,2048]{1,0:T(8,128)(2,1)} %convolution_convert_fusion.3), channel_id=1, source_target_pairs={{16,0},{20,4},{24,8},{28,12},{0,16},{4,20},{8,24},{12,28},{17,1},{... | collective-permute-start | bytes 3145736 | tf_op jit(solution)/shard_map/ppermute | solution.py:111
  283.9 10.2 %all-to-all-start.2 = ((bf16[4,2,2,20,512]{4,2,3,1,0:T(2,128)(2,1)}), bf16[4,2,2,20,512]{4,2,3,1,0:T(2,128)(2,1)S(1)}, u32[]{:S(2)}, u32[]{:S(2)}) async-start(bf16[4,2,2,20,512]{4,2,3,1,0:T(2,128)(2,1)} %copy.112), calls=%async_computation.5 | async-start | bytes 655360 | tf_op jit(solution)/shard_map/all_to_all | solution.py:130
  289.0 38.3 %copy-start.4 = (bf16[1280,512]{1,0:T(8,128)(2,1)S(1)}, bf16[1280,512]{1,0:T(8,128)(2,1)}, u32[]{:S(2)}) copy-start(bf16[1280,512]{1,0:T(8,128)(2,1)} %all-gather.8.cloned.1.call-done) | copy-start | bytes 3932164
Sparse Core Ops, SparseCore 0:
  17.6 37.3 reduce-scatter.5
  58.3 34.6 reduce-scatter.3
  95.1 53.8 all-gather.11
  151.0 53.1 all-gather.9
  213.6 26.1 reduce-scatter.7
  254.9 18.1 all-gather.7

commit v2 on v1

v2 whole, which is shorter than its diff:
```python
import functools
import math

import jax
import jax.numpy as jnp
from jax import lax
from jax.experimental import pallas as pl
from jax.experimental.pallas import tpu as pltpu
from jax.sharding import PartitionSpec as P

K = 5
epsilon = 1e-06


CHUNKS = 4
LANES = 128
STAT_ROWS = 8
MESH = pl.DeviceIdType.MESH


def kernel(
    sizes, weight, draft,
    ctx, ow_hbm, res, place, fcw, goal, gain,
    verified, trained, normed_out, back_out,
    ow, sendp, recvp, hbuf, wbuf, sends, recvs, stat_send, stat_recv, backbuf,
    ow_sem, p_send, p_recv, h_send, h_recv, w_send, w_recv,
    s_send, s_recv, t_send, t_recv, b_send, b_recv, out_sem,
):
    row_count, inner, outer, steps = sizes
    rows, width = res.shape
    half = rows // steps
    chunk = width // CHUNKS
    block = fcw.shape[0]
    me = lax.axis_index("rows")
    column = lax.axis_index("tensor")
    hi = me // inner
    lo = me % inner

    def tensor_peer(j):
        return (me, (column + j) % inner)

    def lo_peer(j):
        return (hi * inner + (lo + j) % inner, column)

    def hi_peer(k):
        return ((me + k * inner) % row_count, column)

    order = [inner // 2] + [j for j in range(1, inner) if j != inner // 2]

    def ow_copy(c, j):
        owner = (column + j) % inner
        start = pl.multiple_of(owner * width + c * chunk, chunk)
        return pltpu.make_async_copy(
            ow_hbm.at[:, pl.ds(start, chunk)], ow.at[c, j], ow_sem.at[c, j]
        )

    for c in range(CHUNKS):
        for j in order + [0]:
            ow_copy(c, j).start()

    barrier = pltpu.get_barrier_semaphore()
    for j in range(1, inner):
        pl.semaphore_signal(barrier, inc=1, device_id=tensor_peer(j), device_id_type=MESH)
        pl.semaphore_signal(barrier, inc=1, device_id=lo_peer(j), device_id_type=MESH)
    for k in range(1, outer):
        pl.semaphore_signal(barrier, inc=1, device_id=hi_peer(k), device_id_type=MESH)
    pl.semaphore_wait(barrier, 2 * (inner - 1) + outer - 1)

    def remote(src, dst, send_sem, recv_sem, device):
        return pltpu.make_async_remote_copy(
            src_ref=src, dst_ref=dst, send_sem=send_sem, recv_sem=recv_sem,
            device_id=device, device_id_type=MESH,
        )

    def w_copy(k):
        return remote(fcw, wbuf.at[k - 1], w_send.at[k - 1], w_recv.at[k - 1], hi_peer(k))

    def p_copy(c, j):
        return remote(
            sendp.at[c, j - 1], recvp.at[c, j - 1], p_send.at[c, j - 1], p_recv.at[c, j - 1],
            tensor_peer(j),
        )

    def h_copy(c, j, owner):
        part = hbuf.at[owner, :, pl.ds(c * chunk, chunk)]
        return remote(part, part, h_send.at[c, j - 1], h_recv.at[c, j - 1], lo_peer(j))

    def s_copy(j):
        return remote(
            sends.at[j - 1], recvs.at[j - 1], s_send.at[j - 1], s_recv.at[j - 1], tensor_peer(j)
        )

    def t_copy(j):
        return remote(
            stat_send, stat_recv.at[j - 1], t_send.at[j - 1], t_recv.at[j - 1], lo_peer(j)
        )

    def b_copy(j, owner):
        return remote(
            backbuf.at[owner], backbuf.at[owner], b_send.at[j - 1], b_recv.at[j - 1],
            tensor_peer(j),
        )

    for k in range(1, outer):
        w_copy(k).start()

    def product(c, j):
        ow_copy(c, j).wait()
        return jnp.dot(ctx[...], ow[c, j], preferred_element_type=jnp.float32).astype(
            jnp.bfloat16
        )

    def finish(c):
        cols = pl.ds(c * chunk, chunk)
        total = product(c, 0).astype(jnp.float32)
        for j in range(1, inner):
            p_copy(c, j).wait_recv()
            total = total + recvp[c, j - 1].astype(jnp.float32)
        total = total + res[:, cols].astype(jnp.float32)
        verified[:, cols] = total
        hidden = total.astype(jnp.bfloat16)
        for step in range(steps):
            hbuf[lo, pl.ds(step * half, half), cols] = jnp.dot(
                place[step], hidden[step * half : (step + 1) * half],
                preferred_element_type=jnp.float32,
            ).astype(jnp.bfloat16)
        for j in range(1, inner):
            h_copy(c, j, lo).start()

    for c in range(CHUNKS):
        for j in order:
            sendp[c, j - 1] = product(c, j)
            p_copy(c, j).start()
        if c >= 1:
            finish(c - 1)
    finish(CHUNKS - 1)

    for j in range(1, inner):
        for c in range(CHUNKS):
            h_copy(c, j, (lo - j + inner) % inner).wait_recv()
    for k in range(1, outer):
        w_copy(k).wait_recv()

    out_copy = pltpu.make_async_copy(hbuf, trained, out_sem)
    out_copy.start()

    def sums(j):
        mine = hbuf[(column + j) % inner]
        parts = [
            lax.dot_general(
                mine, w, (((1,), (1,)), ((), ())), preferred_element_type=jnp.float32
            )
            for w in [fcw[...]] + [wbuf[k - 1] for k in range(1, outer)]
        ]
        return jnp.concatenate(parts, 1).astype(jnp.bfloat16)

    for j in order:
        sends[j - 1] = sums(j)
        s_copy(j).start()
    summed = sums(0).astype(jnp.float32)
    for j in range(1, inner):
        s_copy(j).wait_recv()
        summed = summed + recvs[j - 1].astype(jnp.float32)
    goal_rows = goal[...].astype(jnp.float32)
    gains = gain[...]
    scaled = summed * gains
    lane = lax.broadcasted_iota(jnp.int32, (rows, LANES), 1)
    stats = jnp.where(
        lane == 0,
        jnp.sum(summed * summed, -1, keepdims=True),
        jnp.where(
            lane == 1,
            jnp.sum(scaled * scaled, -1, keepdims=True),
            jnp.sum(scaled * goal_rows, -1, keepdims=True),
        ),
    )
    padded = stat_send.shape[1]
    if padded > rows:
        stats = jnp.concatenate([stats, jnp.zeros((padded - rows, LANES), jnp.float32)], 0)
    stat_send[...] = jnp.transpose(stats)[:STAT_ROWS]
    for j in range(1, inner):
        t_copy(j).start()
    total = stat_send[...]
    for j in range(1, inner):
        t_copy(j).wait_recv()
        total = total + stat_recv[j - 1]
    total = jnp.transpose(
        jnp.concatenate([total, jnp.zeros((LANES - STAT_ROWS, padded), jnp.float32)], 0)
    )[:rows]
    inverse = lax.rsqrt(total[:, 0:1] / draft + epsilon)
    spread = weight * (inverse * total[:, 1:2] - total[:, 2:3]) / draft
    normed = scaled * inverse
    pulled = gains * (weight * (normed - goal_rows))
    backbuf[column] = (inverse * (pulled - summed * (inverse * inverse) * spread)).astype(
        jnp.bfloat16
    )
    for j in range(1, inner):
        b_copy(j, column).start()
    normed_out[...] = normed.astype(jnp.bfloat16)
    for j in range(1, inner):
        b_copy(j, (column - j + inner) % inner).wait_recv()
    back_out[...] = backbuf[...]

    for k in range(1, outer):
        w_copy(k).wait_send()
    for j in range(1, inner):
        for c in range(CHUNKS):
            p_copy(c, j).wait_send()
            h_copy(c, j, lo).wait_send()
        s_copy(j).wait_send()
        t_copy(j).wait_send()
        b_copy(j, column).wait_send()
    out_copy.wait()


def local(context, o_weight, residual, counts, slots, fc_weight, gain, goal):
    steps = context.shape[0]
    row_count = lax.axis_size("rows")
    inner = lax.axis_size("tensor")
    outer = row_count // inner
    rows_dev = context.shape[1]
    width = residual.shape[2]
    block = fc_weight.shape[0]
    draft = goal.shape[2]
    per_peer = rows_dev // row_count
    source = lax.axis_index("rows")
    column = lax.axis_index("tensor")
    hi = source // inner
    lo = source % inner
    weight = 1.0 / math.sqrt(steps * rows_dev * row_count)
    shifts = [
        [(r, (r + k * inner) % row_count) for r in range(row_count)] for k in range(outer)
    ]

    relative = (jnp.arange(outer)[:, None] - jnp.arange(outer)[None, :]) % outer
    goal_part = lax.dynamic_index_in_dim(
        goal.reshape(steps, outer, inner, per_peer, outer, inner, block), column, 2, False
    )
    goal_out = jnp.stack(
        [
            jnp.stack([goal_part[:, h, :, (h - k) % outer] for k in range(outer)], 2)
            for h in range(outer)
        ],
        0,
    )
    goal_out = jnp.transpose(goal_out, (0, 4, 1, 2, 3, 5)).reshape(
        row_count, steps, per_peer, outer * block
    )
    goal_in = lax.all_to_all(goal_out, "rows", split_axis=0, concat_axis=0, tiled=True)
    goal_in = jnp.transpose(goal_in, (1, 0, 2, 3)).reshape(steps * rows_dev, outer * block)
    gain_own = gain.reshape(outer, inner, block)[relative[hi], lo].reshape(1, outer * block)

    offsets = jnp.arange(rows_dev, dtype=jnp.int32) % K
    rows = steps * rows_dev
    place = []
    for step in range(steps):
        accepted = offsets < jnp.repeat(counts[step], K)
        slot_ids = slots[step]
        position = slot_ids // rows_dev * per_peer + slot_ids % rows_dev - source * per_peer
        place.append(
            (position[None, :] == jnp.arange(rows_dev)[:, None]) & accepted[None, :]
        )
    place = jnp.stack(place).astype(jnp.bfloat16)
    chunk = width // CHUNKS
    features = outer * block
    padded = -(-rows // LANES) * LANES
    vmem = pl.BlockSpec(memory_space=pltpu.VMEM)
    anywhere = pl.BlockSpec(memory_space=pl.ANY)
    peers = inner - 1
    dma = pltpu.SemaphoreType.DMA
    bf16 = jnp.bfloat16
    verified, trained, normed, back = pl.pallas_call(
        functools.partial(kernel, (row_count, inner, outer, steps), weight, draft),
        out_shape=(
            jax.ShapeDtypeStruct((rows, width), jnp.float32),
            jax.ShapeDtypeStruct((inner, rows, width), bf16),
            jax.ShapeDtypeStruct((rows, features), bf16),
            jax.ShapeDtypeStruct((inner, rows, features), bf16),
        ),
        in_specs=[vmem, anywhere, vmem, vmem, vmem, vmem, vmem],
        out_specs=(vmem, anywhere, vmem, vmem),
        scratch_shapes=[
            pltpu.VMEM((CHUNKS, inner, context.shape[2], chunk), bf16),
            pltpu.VMEM((CHUNKS, peers, rows, chunk), bf16),
            pltpu.VMEM((CHUNKS, peers, rows, chunk), bf16),
            pltpu.VMEM((inner, rows, width), bf16),
            pltpu.VMEM((max(outer - 1, 1), block, width), bf16),
            pltpu.VMEM((peers, rows, features), bf16),
            pltpu.VMEM((peers, rows, features), bf16),
            pltpu.VMEM((STAT_ROWS, padded), jnp.float32),
            pltpu.VMEM((peers, STAT_ROWS, padded), jnp.float32),
            pltpu.VMEM((inner, rows, features), bf16),
            dma((CHUNKS, inner)),
            dma((CHUNKS, peers)),
            dma((CHUNKS, peers)),
            dma((CHUNKS, peers)),
            dma((CHUNKS, peers)),
            dma((max(outer - 1, 1),)),
            dma((max(outer - 1, 1),)),
            dma((peers,)),
            dma((peers,)),
            dma((peers,)),
            dma((peers,)),
            dma((peers,)),
            dma((peers,)),
            dma,
        ],
        compiler_params=pltpu.CompilerParams(
            collective_id=0, has_side_effects=True, vmem_limit_bytes=56 * 1024 * 1024
        ),
    )(
        context.reshape(rows, context.shape[2]),
        o_weight,
        residual.reshape(rows, width),
        place,
        fc_weight,
        goal_in,
        gain_own,
    )
    trained = trained.reshape(inner * rows, width)
    back = back.reshape(inner * rows, features)
    grad_terms = []
    for k in range(outer):
        grad_terms.append(
            lax.dot_general(
                back[:, k * block : (k + 1) * block],
                trained,
                (((0,), (0,)), ((), ())),
                preferred_element_type=jnp.float32,
            )
        )
    grad = grad_terms[0]
    for k in range(1, outer):
        back_shift = [(b, a) for a, b in shifts[k]]
        grad = grad + lax.ppermute(
            grad_terms[k].astype(jnp.bfloat16), "rows", back_shift
        ).astype(jnp.float32)

    out = normed.reshape(steps, row_count, per_peer, outer * block)
    out = lax.all_to_all(
        jnp.transpose(out, (1, 0, 2, 3)), "rows", split_axis=0, concat_axis=0, tiled=True
    ).reshape(outer, inner, steps, per_peer, outer, block)
    out = jnp.stack(
        [
            jnp.stack([out[h, :, :, :, (h - a) % outer] for a in range(outer)], 0)
            for h in range(outer)
        ],
        0,
    )
    out = jnp.transpose(out, (1, 2, 5, 3, 0, 4))
    out = jnp.transpose(
        out.reshape(inner, draft // inner, steps, outer, per_peer), (0, 2, 3, 4, 1)
    )
    out = lax.all_to_all(out, "tensor", split_axis=0, concat_axis=0, tiled=True)
    draft_out = (
        jnp.transpose(out, (1, 2, 0, 3, 4))
        .reshape(steps, rows_dev, draft // inner)
        .astype(jnp.float32)
    )
    return (verified.reshape(steps, rows_dev, width), draft_out, grad)


def solution(mesh):
    placed = (
        P(None, "rows", "tensor"),
        P("tensor", None),
        P(None, "rows", "tensor"),
        P(None, "rows"),
        P(None, "rows"),
        P("rows", "tensor"),
        P(),
        P(None, "rows", None),
    )
    return jax.shard_map(
        local,
        mesh=mesh,
        in_specs=placed,
        out_specs=(P(None, "rows", "tensor"), P(None, "rows", "tensor"), P("rows", "tensor")),
        check_vma=False,
    )
```

time: 341 us -> 228 us (0.67)
  waiting for transfers between devices: 229 us -> 44.8 us
  Pallas kernels: 0 us -> 137 us
  matrix products: 39.9 us -> 10.3 us
  between operations: 14.5 us -> 0.93 us
  blocking collectives: 11.5 us -> 0 us
  other arithmetic: 12.1 us -> 2.46 us
    pallas_call x0 -> x1, Pallas kernels: none -> 137 us  [local(): pl.pallas_call(functools.partial(kernel, (row_count, inner, outer, steps)...]
    all_gather x3 -> x0, waiting for transfers between devices: 108 us -> none  [the longest x2 106 us: local(): lax.all_gather(moved, 'rows', axis=0, tiled=False, axis_index_groups=groups)]
    reduce_scatter x3 -> x0, waiting for transfers between devices: 67.6 us -> none  [the longest x2 60.8 us: local(): lax.psum_scatter(head_terms.astype(jnp.bfloat16), 'tensor', scatter_dimen...]
    dot_general x5 -> x0, matrix products: 29 us -> none  [the longest x2 20.4 us: local(): jnp.dot(context[step], o_weight, preferred_element_type=jnp.float32)]
    ppermute x1, waiting for transfers between devices: 31.5 us -> 6.81 us  [local(): lax.ppermute(grad_terms[k].astype(jnp.bfloat16), 'rows', back_shift)]
    all_to_all x1, waiting for transfers between devices: 6.63 us -> 23.4 us  [local(): lax.all_to_all(jnp.transpose(out, (1, 0, 2, 3)), 'rows', split_axis=0, co...]
    all_gather x1 -> x0, blocking collectives: 11.5 us -> none  [local(): lax.all_gather(stats, 'rows', axis=0, tiled=False, axis_index_groups=groups)]
    another operation x3 -> x0, other arithmetic: 6.8 us -> none  [the longest x2 3.79 us: local(): return (jnp.stack(verified), draft_out, grad)]
  transfers between devices with their start and end apart: 11 -> 4, of which waited for: 10 -> 4; matrix products, arithmetic and copies ran while one was open for 10% -> 5% of each run, Pallas kernels for 0% -> 0%
where the time goes in v2:
time: 228 us; the launch traced here: 227 us
  Pallas kernels  137 us (60%)
  waiting for transfers between devices  44.8 us (20%)
  starting transfers between devices  17 us (7%)
  local copies, waits for them, and re-layouts  14.7 us (6%)
  matrix products  10.3 us (5%)
  other arithmetic  2.46 us (1%)
    pallas_call x1, Pallas kernels, local(): pl.pallas_call(functools.partial(kernel, (row_count, inner, outer, steps)...  137 us
    all_to_all x1, waiting for transfers between devices, local(): lax.all_to_all(jnp.transpose(out, (1, 0, 2, 3)), 'rows', split_axis=0, co...  23.4 us
    dot_general x2, matrix products, local(): lax.dot_general(back[:, k * block:(k + 1) * block], trained, (((0,), (0,)...  10.3 us
    all_to_all x1, waiting for transfers between devices, local(): lax.all_to_all(goal_out, 'rows', split_axis=0, concat_axis=0, tiled=True)  7.87 us
    all_to_all x1, starting transfers between devices, local(): lax.all_to_all(goal_out, 'rows', split_axis=0, concat_axis=0, tiled=True)  7.25 us
    ppermute x1, waiting for transfers between devices, local(): lax.ppermute(grad_terms[k].astype(jnp.bfloat16), 'rows', back_shift)  6.81 us
    all_to_all x1, waiting for transfers between devices, local(): out = lax.all_to_all(out, 'tensor', split_axis=0, concat_axis=0, tiled=True)  6.7 us
  transfers between devices with their start and end apart: 4, of which 4 were waited for; matrix products, arithmetic and copies ran while one was open for 5% of the time, Pallas kernels for 0%

profile of v2, /device:TPU:0, one launch (start us, length us, event | category | flops | bytes accessed | tf_op | source)
XLA Modules:
  0.0 227.4 jit_solution(16215771433570203100)
XLA Ops:
  0.6 3.2 %reshape.221 = bf16[2,2,4,20,2,4,256]{6,5,4,3,2,1,0:T(4,128)(2,1)S(1)} reshape(bf16[2,160,2048]{2,1,0:T(8,128)(2,1)} %param.15) | data formatting | bytes 2621440 | tf_op jit(solution)/shard_map/reshape | solution.py:237
  4.2 0.2 maximum_bitcast_fusion.2
  4.4 0.2 maximum_bitcast_fusion
  4.6 0.3 copy.103
  5.0 0.9 reshape.239
  5.9 7.3 %all-to-all-start = ((bf16[8,2,20,512]{3,1,2,0:T(2,128)(2,1)}), bf16[8,2,20,512]{3,1,2,0:T(2,128)(2,1)S(1)}, u32[]{:S(2)}, u32[]{:S(2)}) async-start(bf16[8,2,20,512]{3,1,2,0:T(2,128)(2,1)} %reshape.239), calls=%async_computation | async-start | bytes 655360 | tf_op jit(solution)/shard_map/all_to_all | solution.py:249
  13.7 0.6 gather_fusion
  14.2 0.6 copy.117
  14.9 0.7 add_convert_fusion.place
  15.6 7.9 %all-to-all-done = bf16[8,2,20,512]{3,1,2,0:T(2,128)(2,1)S(1)} async-done(((bf16[8,2,20,512]{3,1,2,0:T(2,128)(2,1)}), bf16[8,2,20,512]{3,1,2,0:T(2,128)(2,1)S(1)}, u32[]{:S(2)}, u32[]{:S(2)}) %all-to-all-start) | async-done | bytes 327712 | tf_op jit(solution)/shard_map/all_to_all | solution.py:249
  23.5 0.8 reshape.223.goal
  24.3 137.3 %shard_map.103 = (f32[320,2048]{1,0:T(8,128)}, bf16[4,320,2048]{2,1,0:T(8,128)(2,1)}, bf16[320,512]{1,0:T(8,128)(2,1)}, bf16[4,320,512]{2,1,0:T(8,128)(2,1)}) custom-call(bf16[320,1024]{1,0:T(8,128)(2,1)} %bitcast.82, bf16[1024,8192]{1,0:T(8,128)(2,1)} %ow_hbm.1, bf16[320,2048]{1,0:T(8,128)(2,1)} %bitcast.79, bf16[2,160,160]{2,1,0:T(8,128)(2,1)} %add_convert_fusion.place, ...), custom_call_target="tpu_custom_call" | custom-call | tf_op jit(solution)/shard_map/pallas_call | solution.py:272
  161.6 1.1 reshape.227
  162.8 1.1 copy.93
  163.8 3.7 %all-to-all-start.1 = ((bf16[8,2,20,512]{3,1,2,0:T(2,128)(2,1)}), bf16[8,2,20,512]{3,1,2,0:T(2,128)(2,1)S(1)}, u32[]{:S(2)}, u32[]{:S(2)}) async-start(bf16[8,2,20,512]{3,1,2,0:T(2,128)(2,1)} %copy.93), calls=%async_computation.1 | async-start | bytes 655360 | tf_op jit(solution)/shard_map/all_to_all | solution.py:340
  167.5 5.0 %convolution_convert_fusion = bf16[256,2048]{1,0:T(8,128)(2,1)} fusion(bf16[1280,2048]{1,0:T(8,128)(2,1)} %bitcast.72, bf16[1280,512]{1,0:T(8,128)(2,1)S(1)} %bitcast.80), kind=kOutput, calls=%fused_computation.1 | convolution fusion | flops 1342701568 | bytes 6946816 | tf_op jit(solution)/shard_map/dot_general | solution.py:325
  172.5 2.6 %collective-permute-start = (bf16[256,2048]{1,0:T(8,128)(2,1)}, bf16[256,2048]{1,0:T(8,128)(2,1)S(1)}, u32[]{:S(2)}, u32[]{:S(2)}) collective-permute-start(bf16[256,2048]{1,0:T(8,128)(2,1)} %convolution_convert_fusion), channel_id=1, source_target_pairs={{16,0},{20,4},{24,8},{28,12},{0,16},{4,20},{8,24},{12,28},{17,1},{... | collective-permute-start | bytes 3145736 | tf_op jit(solution)/shard_map/ppermute | solution.py:335
  175.1 23.4 %all-to-all-done.1 = bf16[8,2,20,512]{3,1,2,0:T(2,128)(2,1)S(1)} async-done(((bf16[8,2,20,512]{3,1,2,0:T(2,128)(2,1)}), bf16[8,2,20,512]{3,1,2,0:T(2,128)(2,1)S(1)}, u32[]{:S(2)}, u32[]{:S(2)}) %all-to-all-start.1) | async-done | bytes 327712 | tf_op jit(solution)/shard_map/all_to_all | solution.py:340
  198.7 0.5 fusion.18
  199.5 0.2 maximum_bitcast_fusion.4
  199.8 0.2 maximum_bitcast_fusion.5
  200.0 0.5 maximum_bitcast_fusion.1
  200.6 0.2 reshape.229
  200.8 1.1 copy.100
  201.9 3.5 %all-to-all-start.2 = ((bf16[4,2,2,20,512]{4,2,3,1,0:T(2,128)(2,1)}), bf16[4,2,2,20,512]{4,2,3,1,0:T(2,128)(2,1)S(1)}, u32[]{:S(2)}, u32[]{:S(2)}) async-start(bf16[4,2,2,20,512]{4,2,3,1,0:T(2,128)(2,1)} %copy.100), calls=%async_computation.2 | async-start | bytes 655360 | tf_op jit(solution)/shard_map/all_to_all | solution.py:354
  205.4 6.7 %all-to-all-done.2 = bf16[4,2,2,20,512]{4,2,3,1,0:T(2,128)(2,1)S(1)} async-done(((bf16[4,2,2,20,512]{4,2,3,1,0:T(2,128)(2,1)}), bf16[4,2,2,20,512]{4,2,3,1,0:T(2,128)(2,1)S(1)}, u32[]{:S(2)}, u32[]{:S(2)}) %all-to-all-start.2) | async-done | bytes 327712 | tf_op jit(solution)/shard_map/all_to_all | solution.py:354
  212.1 0.2 convert_bitcast_fusion
  212.3 0.5 copy.101
  212.8 1.0 copy.102
  213.8 6.8 %collective-permute-done = bf16[256,2048]{1,0:T(8,128)(2,1)S(1)} collective-permute-done((bf16[256,2048]{1,0:T(8,128)(2,1)}, bf16[256,2048]{1,0:T(8,128)(2,1)S(1)}, u32[]{:S(2)}, u32[]{:S(2)}) %collective-permute-start) | collective-permute-done | bytes 1048608 | tf_op jit(solution)/shard_map/ppermute | solution.py:335
  220.6 5.3 %convert_add_fusion = f32[256,2048]{1,0:T(8,128)} fusion(bf16[256,2048]{1,0:T(8,128)(2,1)S(1)} %collective-permute-done, bf16[1280,2048]{1,0:T(8,128)(2,1)} %bitcast.73, bf16[1280,512]{1,0:T(8,128)(2,1)S(1)} %bitcast.81), kind=kOutput, calls=%fused_computation.2 | convolution fusion | flops 1343225856 | bytes 9043968 | tf_op jit(solution)/shard_map/dot_general | solution.py:325
  225.9 1.5 copy.127
  (31 shorter events, 1.5 us)
Async XLA Ops:
  4.0 9.2 %copy-start.4 = (s32[2,32]{1,0:T(2,128)S(1)}, s32[2,32]{1,0:T(2,128)}, u32[]{:S(2)}) copy-start(s32[2,32]{1,0:T(2,128)} %param.11) | copy-start | bytes 772
  4.0 9.6 %copy-start.2 = (f32[2048]{0:T(1024)S(1)}, f32[2048]{0:T(1024)}, u32[]{:S(2)}) copy-start(f32[2048]{0:T(1024)} %param.14) | copy-start | bytes 24580
  4.0 10.8 %copy-start.3 = (s32[2,160]{1,0:T(2,128)S(1)}, s32[2,160]{1,0:T(2,128)}, u32[]{:S(2)}) copy-start(s32[2,160]{1,0:T(2,128)} %param.12) | copy-start | bytes 3844
  5.9 17.6 %all-to-all-start = ((bf16[8,2,20,512]{3,1,2,0:T(2,128)(2,1)}), bf16[8,2,20,512]{3,1,2,0:T(2,128)(2,1)S(1)}, u32[]{:S(2)}, u32[]{:S(2)}) async-start(bf16[8,2,20,512]{3,1,2,0:T(2,128)(2,1)} %reshape.239), calls=%async_computation | async-start | bytes 655360 | tf_op jit(solution)/shard_map/all_to_all | solution.py:249
  161.6 5.9 %copy-start.1 = (bf16[4,320,512]{2,1,0:T(8,128)(2,1)S(1)}, bf16[4,320,512]{2,1,0:T(8,128)(2,1)}, u32[]{:S(2)}) copy-start(bf16[4,320,512]{2,1,0:T(8,128)(2,1)} %get-tuple-element.9) | copy-start | bytes 3932164
  163.8 34.7 %all-to-all-start.1 = ((bf16[8,2,20,512]{3,1,2,0:T(2,128)(2,1)}), bf16[8,2,20,512]{3,1,2,0:T(2,128)(2,1)S(1)}, u32[]{:S(2)}, u32[]{:S(2)}) async-start(bf16[8,2,20,512]{3,1,2,0:T(2,128)(2,1)} %copy.93), calls=%async_computation.1 | async-start | bytes 655360 | tf_op jit(solution)/shard_map/all_to_all | solution.py:340
  172.5 48.1 %collective-permute-start = (bf16[256,2048]{1,0:T(8,128)(2,1)}, bf16[256,2048]{1,0:T(8,128)(2,1)S(1)}, u32[]{:S(2)}, u32[]{:S(2)}) collective-permute-start(bf16[256,2048]{1,0:T(8,128)(2,1)} %convolution_convert_fusion), channel_id=1, source_target_pairs={{16,0},{20,4},{24,8},{28,12},{0,16},{4,20},{8,24},{12,28},{17,1},{... | collective-permute-start | bytes 3145736 | tf_op jit(solution)/shard_map/ppermute | solution.py:335
  201.9 10.2 %all-to-all-start.2 = ((bf16[4,2,2,20,512]{4,2,3,1,0:T(2,128)(2,1)}), bf16[4,2,2,20,512]{4,2,3,1,0:T(2,128)(2,1)S(1)}, u32[]{:S(2)}, u32[]{:S(2)}) async-start(bf16[4,2,2,20,512]{4,2,3,1,0:T(2,128)(2,1)} %copy.100), calls=%async_computation.2 | async-start | bytes 655360 | tf_op jit(solution)/shard_map/all_to_all | solution.py:354
  213.8 12.2 %copy-start = (f32[320,2048]{1,0:T(8,128)S(1)}, f32[320,2048]{1,0:T(8,128)}, u32[]{:S(2)}) copy-start(f32[320,2048]{1,0:T(8,128)} %get-tuple-element.7) | copy-start | bytes 7864324

commit v3 on v2

--- a/solution.py
+++ b/solution.py
@@ -3,6 +3,7 @@
 
 import jax
 import jax.numpy as jnp
+import numpy as np
 from jax import lax
 from jax.experimental import pallas as pl
 from jax.experimental.pallas import tpu as pltpu
@@ -20,11 +21,13 @@
 
 def kernel(
     sizes, weight, draft,
-    ctx, ow_hbm, res, place, fcw, goal, gain,
-    verified, trained, normed_out, back_out,
+    ctx, ow_hbm, res, place, fcw, goal, gain, pick,
+    verified, grad, out_final,
     ow, sendp, recvp, hbuf, wbuf, sends, recvs, stat_send, stat_recv, backbuf,
     ow_sem, p_send, p_recv, h_send, h_recv, w_send, w_recv,
-    s_send, s_recv, t_send, t_recv, b_send, b_recv, out_sem,
+    s_send, s_recv, t_send, t_recv, b_send, b_recv,
+    goalbuf, out_rows, out_in, out_last, gsend, grecv,
+    goal_send, goal_recv, r_send, r_recv, f_send, f_recv, g_send, g_recv, own_sem, last_sem,
 ):
     row_count, inner, outer, steps = sizes
     rows, width = res.shape
@@ -45,6 +48,9 @@
     def hi_peer(k):
         return ((me + k * inner) % row_count, column)
 
+    def row_peer(d):
+        return ((me + d) % row_count, column)
+
     order = [inner // 2] + [j for j in range(1, inner) if j != inner // 2]
 
     def ow_copy(c, j):
@@ -61,10 +67,9 @@
     barrier = pltpu.get_barrier_semaphore()
     for j in range(1, inner):
         pl.semaphore_signal(barrier, inc=1, device_id=tensor_peer(j), device_id_type=MESH)
-        pl.semaphore_signal(barrier, inc=1, device_id=lo_peer(j), device_id_type=MESH)
-    for k in range(1, outer):
-        pl.semaphore_signal(barrier, inc=1, device_id=hi_peer(k), device_id_type=MESH)
-    pl.semaphore_wait(barrier, 2 * (inner - 1) + outer - 1)
+    for d in range(1, row_count):
+        pl.semaphore_signal(barrier, inc=1, device_id=row_peer(d), device_id_type=MESH)
+    pl.semaphore_wait(barrier, inner + row_count - 2)
 
     def remote(src, dst, send_sem, recv_sem, device):
         return pltpu.make_async_remote_copy(
@@ -101,6 +106,43 @@
             tensor_peer(j),
         )
 
+    slot = goal.shape[1]
+    per_owner = out_final.shape[2]
+
+    def goal_copy(d, landing):
+        return remote(
+            goal.at[(me + d) % row_count], goalbuf.at[landing],
+            goal_send.at[d - 1], goal_recv.at[d - 1], row_peer(d),
+        )
+
+    def r_copy(d, landing):
+        return remote(
+            out_rows.at[(me + d) % row_count], out_in.at[landing],
+            r_send.at[d - 1], r_recv.at[d - 1], row_peer(d),
+        )
+
+    def final_source(j, h, sub):
+        first = per_owner * ((column + j) % inner)
+        return out_in.at[
+            h * inner + first % inner + sub, (h - first // inner + outer) % outer
+        ]
+
+    def f_copy(j, h, sub, landing):
+        return remote(
+            final_source(j, h, sub), out_last.at[landing, h, sub],
+            f_send.at[j - 1, h, sub], f_recv.at[j - 1, h, sub], tensor_peer(j),
+        )
+
+    def g_copy(k, c):
+        return remote(
+            gsend.at[k - 1, c], grecv.at[k - 1, c], g_send.at[k - 1, c], g_recv.at[k - 1, c],
+            ((me - k * inner + row_count) % row_count, column),
+        )
+
+    own_goal = pltpu.make_async_copy(goal.at[me], goalbuf.at[me], own_sem.at[0])
+    own_goal.start()
+    for d in range(1, row_count):
+        goal_copy(d, me).start()
     for k in range(1, outer):
         w_copy(k).start()
 
@@ -141,9 +183,6 @@
     for k in range(1, outer):
         w_copy(k).wait_recv()
 
-    out_copy = pltpu.make_async_copy(hbuf, trained, out_sem)
-    out_copy.start()
-
     def sums(j):
         mine = hbuf[(column + j) % inner]
         parts = [
@@ -161,7 +200,14 @@
     for j in range(1, inner):
         s_copy(j).wait_recv()
         summed = summed + recvs[j - 1].astype(jnp.float32)
-    goal_rows = goal[...].astype(jnp.float32)
+    own_goal.wait()
+    for d in range(1, row_count):
+        goal_copy(d, (me - d + row_count) % row_count).wait_recv()
+    goal_rows = jnp.dot(
+        pick[...],
+        goalbuf[...].reshape(row_count * slot, goal.shape[2]),
+        preferred_element_type=jnp.float32,
+    )
     gains = gain[...]
     scaled = summed * gains
     lane = lax.broadcasted_iota(jnp.int32, (rows, LANES), 1)
@@ -196,11 +242,74 @@
     )
     for j in range(1, inner):
         b_copy(j, column).start()
-    normed_out[...] = normed.astype(jnp.bfloat16)
+    rounded = normed.astype(jnp.bfloat16)
+    for k in range(outer):
+        out_rows[:, k] = (
+            lax.dot_general(
+                pick[...], rounded[:, k * block : (k + 1) * block],
+                (((0,), (0,)), ((), ())), preferred_element_type=jnp.float32,
+            )
+            .astype(jnp.bfloat16)
+            .reshape(row_count, slot, block)
+        )
     for j in range(1, inner):
         b_copy(j, (column - j + inner) % inner).wait_recv()
-    back_out[...] = backbuf[...]
-
+    back = backbuf[...].reshape(inner * rows, outer * block)
+
+    def gradient(k, c):
+        inputs = hbuf[:, :, c * chunk : (c + 1) * chunk].reshape(inner * rows, chunk)
+        return lax.dot_general(
+            back[:, k * block : (k + 1) * block], inputs,
+            (((0,), (0,)), ((), ())), preferred_element_type=jnp.float32,
+        )
+
+    for c in range(CHUNKS):
+        for k in range(1, outer):
+            gsend[k - 1, c] = gradient(k, c).astype(jnp.bfloat16)
+            g_copy(k, c).start()
+        if c == 0:
+            own_rows = pltpu.make_async_copy(out_rows.at[me], out_in.at[me], own_sem.at[1])
+            own_rows.start()
+            for d in range(1, row_count):
+                r_copy(d, me).start()
+    for c in range(CHUNKS):
+        grad[:, c * chunk : (c + 1) * chunk] = gradient(0, c)
+    own_rows.wait()
+    for d in range(1, row_count):
+        r_copy(d, (me - d + row_count) % row_count).wait_recv()
+    own_last = []
+    for h in range(outer):
+        for sub in range(per_owner):
+            own_last.append(
+                pltpu.make_async_copy(
+                    final_source(0, h, sub), out_last.at[column, h, sub], last_sem.at[h, sub]
+                )
+            )
+            own_last[-1].start()
+            for j in range(1, inner):
+                f_copy(j, h, sub, column).start()
+    for c in range(CHUNKS):
+        cols = pl.ds(c * chunk, chunk)
+        part = grad[:, cols]
+        for k in range(1, outer):
+            g_copy(k, c).wait_recv()
+            part = part + grecv[k - 1, c].astype(jnp.float32)
+        grad[:, cols] = part
+    for copy in own_last:
+        copy.wait()
+    for j in range(1, inner):
+        for h in range(outer):
+            for sub in range(per_owner):
+                f_copy(j, h, sub, (column - j + inner) % inner).wait_recv()
+                f_copy(j, h, sub, column).wait_send()
+    out_final[...] = out_last[...]
+
+    for d in range(1, row_count):
+        goal_copy(d, me).wait_send()
+        r_copy(d, me).wait_send()
+    for k in range(1, outer):
+        for c in range(CHUNKS):
+            g_copy(k, c).wait_send()
     for k in range(1, outer):
         w_copy(k).wait_send()
     for j in range(1, inner):
@@ -210,7 +319,6 @@
         s_copy(j).wait_send()
         t_copy(j).wait_send()
         b_copy(j, column).wait_send()
-    out_copy.wait()
 
 
 def local(context, o_weight, residual, counts, slots, fc_weight, gain, goal):
@@ -228,9 +336,6 @@
     hi = source // inner
     lo = source % inner
     weight = 1.0 / math.sqrt(steps * rows_dev * row_count)
-    shifts = [
-        [(r, (r + k * inner) % row_count) for r in range(row_count)] for k in range(outer)
-    ]
 
     relative = (jnp.arange(outer)[:, None] - jnp.arange(outer)[None, :]) % outer
     goal_part = lax.dynamic_index_in_dim(
@@ -243,11 +348,15 @@
         ],
         0,
     )
-    goal_out = jnp.transpose(goal_out, (0, 4, 1, 2, 3, 5)).reshape(
-        row_count, steps, per_peer, outer * block
-    )
-    goal_in = lax.all_to_all(goal_out, "rows", split_axis=0, concat_axis=0, tiled=True)
-    goal_in = jnp.transpose(goal_in, (1, 0, 2, 3)).reshape(steps * rows_dev, outer * block)
+    goal_out = jnp.transpose(goal_out, (0, 4, 1, 2, 3, 5))
+    slot = -(-steps * per_peer // 16) * 16
+    goal_out = jnp.pad(
+        goal_out.reshape(row_count, steps * per_peer, outer * block),
+        ((0, 0), (0, slot - steps * per_peer), (0, 0)),
+    )
+    index = np.arange(steps * rows_dev)
+    where = index % rows_dev // per_peer * slot + index // rows_dev * per_peer + index % per_peer
+    pick = jnp.asarray(where[:, None] == np.arange(row_count * slot)[None, :], jnp.bfloat16)
     gain_own = gain.reshape(outer, inner, block)[relative[hi], lo].reshape(1, outer * block)
 
     offsets = jnp.arange(rows_dev, dtype=jnp.int32) % K
@@ -269,16 +378,17 @@
     peers = inner - 1
     dma = pltpu.SemaphoreType.DMA
     bf16 = jnp.bfloat16
-    verified, trained, normed, back = pl.pallas_call(
+    per_owner = draft // inner // block
+    between = max(outer - 1, 1)
+    verified, grad, out = pl.pallas_call(
         functools.partial(kernel, (row_count, inner, outer, steps), weight, draft),
         out_shape=(
             jax.ShapeDtypeStruct((rows, width), jnp.float32),
-            jax.ShapeDtypeStruct((inner, rows, width), bf16),
-            jax.ShapeDtypeStruct((rows, features), bf16),
-            jax.ShapeDtypeStruct((inner, rows, features), bf16),
+            jax.ShapeDtypeStruct((block, width), jnp.float32),
+            jax.ShapeDtypeStruct((inner, outer, per_owner, slot, block), bf16),
         ),
-        in_specs=[vmem, anywhere, vmem, vmem, vmem, vmem, vmem],
-        out_specs=(vmem, anywhere, vmem, vmem),
+        in_specs=[vmem, anywhere, vmem, vmem, vmem, vmem, vmem, vmem],
+        out_specs=(vmem, vmem, vmem),
         scratch_shapes=[
             pltpu.VMEM((CHUNKS, inner, context.shape[2], chunk), bf16),
             pltpu.VMEM((CHUNKS, peers, rows, chunk), bf16),
@@ -303,7 +413,22 @@
             dma((peers,)),
             dma((peers,)),
             dma((peers,)),
-            dma,
+            pltpu.VMEM((row_count, slot, features), bf16),
+            pltpu.VMEM((row_count, outer, slot, block), bf16),
+            pltpu.VMEM((row_count, outer, slot, block), bf16),
+            pltpu.VMEM((inner, outer, per_owner, slot, block), bf16),
+            pltpu.VMEM((between, CHUNKS, block, chunk), bf16),
+            pltpu.VMEM((between, CHUNKS, block, chunk), bf16),
+            dma((row_count - 1,)),
+            dma((row_count - 1,)),
+            dma((row_count - 1,)),
+            dma((row_count - 1,)),
+            dma((peers, outer, per_owner)),
+            dma((peers, outer, per_owner)),
+            dma((between, CHUNKS)),
+            dma((between, CHUNKS)),
+            dma((2,)),
+            dma((outer, per_owner)),
         ],
         compiler_params=pltpu.CompilerParams(
             collective_id=0, has_side_effects=True, vmem_limit_bytes=56 * 1024 * 1024
@@ -314,46 +439,15 @@
         residual.reshape(rows, width),
         place,
         fc_weight,
-        goal_in,
+        goal_out,
         gain_own,
-    )
-    trained = trained.reshape(inner * rows, width)
-    back = back.reshape(inner * rows, features)
-    grad_terms = []
-    for k in range(outer):
-        grad_terms.append(
-            lax.dot_general(
-                back[:, k * block : (k + 1) * block],
-                trained,
-                (((0,), (0,)), ((), ())),
-                preferred_element_type=jnp.float32,
-            )
-        )
-    grad = grad_terms[0]
-    for k in range(1, outer):
-        back_shift = [(b, a) for a, b in shifts[k]]
-        grad = grad + lax.ppermute(
-            grad_terms[k].astype(jnp.bfloat16), "rows", back_shift
-        ).astype(jnp.float32)
-
-    out = normed.reshape(steps, row_count, per_peer, outer * block)
-    out = lax.all_to_all(
-        jnp.transpose(out, (1, 0, 2, 3)), "rows", split_axis=0, concat_axis=0, tiled=True
-    ).reshape(outer, inner, steps, per_peer, outer, block)
-    out = jnp.stack(
-        [
-            jnp.stack([out[h, :, :, :, (h - a) % outer] for a in range(outer)], 0)
-            for h in range(outer)
-        ],
-        0,
-    )
-    out = jnp.transpose(out, (1, 2, 5, 3, 0, 4))
-    out = jnp.transpose(
-        out.reshape(inner, draft // inner, steps, outer, per_peer), (0, 2, 3, 4, 1)
-    )
-    out = lax.all_to_all(out, "tensor", split_axis=0, concat_axis=0, tiled=True)
+        pick,
+    )
+    out = out[:, :, :, : steps * per_peer].reshape(
+        inner, outer, per_owner, steps, per_peer, block
+    )
     draft_out = (
-        jnp.transpose(out, (1, 2, 0, 3, 4))
+        jnp.transpose(out, (3, 1, 0, 4, 2, 5))
         .reshape(steps, rows_dev, draft // inner)
         .astype(jnp.float32)
     )

time: 228 us -> 215 us (0.943)
  Pallas kernels: 137 us -> 197 us
  waiting for transfers between devices: 44.8 us -> 0 us
  starting transfers between devices: 17 us -> 0 us
  matrix products: 10.3 us -> 0 us
    pallas_call x1, Pallas kernels: 137 us -> 197 us  [local(): pl.pallas_call(functools.partial(kernel, (row_count, inner, outer, steps)...]
    all_to_all x3 -> x0, waiting for transfers between devices: 38 us -> none  [the longest x1 23.4 us: local(): lax.all_to_all(jnp.transpose(out, (1, 0, 2, 3)), 'rows', split_axis=0, co...]
    all_to_all x3 -> x0, starting transfers between devices: 14.4 us -> none  [the longest x1 7.25 us: local(): lax.all_to_all(goal_out, 'rows', split_axis=0, concat_axis=0, tiled=True)]
    dot_general x2 -> x0, matrix products: 10.3 us -> none  [local(): lax.dot_general(back[:, k * block:(k + 1) * block], trained, (((0,), (0,)...]
    ppermute x1 -> x0, waiting for transfers between devices: 6.81 us -> none  [local(): lax.ppermute(grad_terms[k].astype(jnp.bfloat16), 'rows', back_shift)]
    reshape x6 -> x1, local copies, waits for them, and re-layouts: 3.63 us -> 0.21 us  [local(): goal_out.reshape(row_count, steps * per_peer, outer * block)]
    ppermute x1 -> x0, starting transfers between devices: 2.61 us -> none  [local(): lax.ppermute(grad_terms[k].astype(jnp.bfloat16), 'rows', back_shift)]
  transfers between devices with their start and end apart: 4 -> 0, of which waited for: 4 -> 0; matrix products, arithmetic and copies ran while one was open for 5% -> 0% of each run, Pallas kernels for 0% -> 0%
where the time goes in v3:
time: 215 us; the launch traced here: 214 us
  Pallas kernels  197 us (92%)
  local copies, waits for them, and re-layouts  13.6 us (6%)
  other arithmetic  3.09 us (1%)
    pallas_call x1, Pallas kernels, local(): pl.pallas_call(functools.partial(kernel, (row_count, inner, outer, steps)...  197 us
    unnamed x7, local copies, waits for them, and re-layouts  4.44 us

profile of v3, /device:TPU:0, one launch (start us, length us, event | category | flops | bytes accessed | tf_op | source)
XLA Modules:
  0.0 214.4 jit_solution(6270479481623429475)
XLA Ops:
  0.7 0.8 slice_bitcast_fusion.5
  1.5 0.8 fusion.6
  2.2 0.7 reshape.208
  3.0 0.6 gather_fusion
  3.5 0.6 copy.24
  4.1 0.1 broadcast_in_dim.4
  4.2 0.1 reshape.204
  4.3 0.1 broadcast_in_dim.5
  4.4 0.1 reshape.205
  4.5 0.1 fusion
  4.6 0.7 add_convert_fusion.place
  5.3 3.2 %reshape.206 = bf16[2,2,4,20,2,4,256]{6,5,4,3,2,1,0:T(4,128)(2,1)S(1)} reshape(bf16[2,160,2048]{2,1,0:T(8,128)(2,1)} %param.16) | data formatting | bytes 2621440 | tf_op jit(solution)/shard_map/reshape | solution.py:342
  8.5 0.1 copy_bitcast_fusion
  8.6 0.1 slice_bitcast_fusion.3
  8.8 0.2 maximum_bitcast_fusion.1
  9.0 0.2 maximum_bitcast_fusion
  9.2 0.3 copy.20
  9.6 0.2 reshape.207
  9.8 0.8 pad.5.goal
  10.6 197.0 %shard_map.112 = (f32[320,2048]{1,0:T(8,128)}, f32[256,2048]{1,0:T(8,128)}, bf16[4,2,2,48,256]{4,3,2,1,0:T(8,128)(2,1)}) custom-call(bf16[320,1024]{1,0:T(8,128)(2,1)} %bitcast.38, bf16[1024,8192]{1,0:T(8,128)(2,1)} %ow_hbm.1, bf16[320,2048]{1,0:T(8,128)(2,1)} %bitcast.37, bf16[2,160,160]{2,1,0:T(8,128)(2,1)} %add_convert_fusion.place, ...), custom_call_target="tpu_custom_call" | custom-call | tf_op jit(solution)/shard_map/pallas_call | solution.py:383
  207.6 1.0 slice_convert_fusion
  208.6 0.0 copy-start
  208.6 0.3 copy.21
  209.0 0.2 copy.22
  209.2 1.4 reshape.211
  210.6 0.0 copy-done
  210.6 0.0 copy-start.1
  210.6 1.5 copy.28
  212.1 1.0 copy-done.1
  213.1 1.3 copy.29
  (4 shorter events, 0.1 us)
Async XLA Ops:
  208.6 2.0 copy-start
  210.6 2.5 %copy-start.1 = (f32[256,2048]{1,0:T(8,128)S(1)}, f32[256,2048]{1,0:T(8,128)}, u32[]{:S(2)}) copy-start(f32[256,2048]{1,0:T(8,128)} %get-tuple-element.26) | copy-start | bytes 6291460
